TPU v7x, 1024 devices: a whole 8x8x8 slice. The times are simulated.
1024 devices in a mesh: fsdp: 128 (over z, y, x_hi), tp: 8 (over x_lo, core).
Axes of the slice: x: 8 (x_hi: 2, x_lo: 4; x = x_hi * 4 + x_lo), y: 8, z: 8, core: 2. Of those that a mesh axis runs over, the one named last changes fastest.
Arguments:
- hidden: bfloat16 [2, 9216, 16384], P(None, 'fsdp', 'tp'), may hold values from -6 to 6
- queries: bfloat16 [2, 9216, 16384], P(None, 'fsdp', 'tp'), may hold values from -256 to 256
- cache_keys: bfloat16 [9216, 32, 1024], P('fsdp', None, 'tp'), may hold values from -6 to 6
- cache_values: bfloat16 [9216, 32, 1024], P('fsdp', None, 'tp'), may hold values from -6 to 6
- new_values: bfloat16 [2, 9216, 1024], P(None, 'fsdp', 'tp'), may hold values from -6 to 6
- lengths: int32 [9216], P('fsdp'), may hold values from 2 to 32, as said below
- base_weight: bfloat16 [16384, 1024], P(None, 'tp'), may hold values from -0.046875 to 0.046875
- delta_values: bfloat16 [16384, 1024], P(('fsdp', 'tp')), may hold values from -4 to 4
- delta_scales: bfloat16 [128, 8], P('fsdp', 'tp'), may hold values from 0.0019989014 to 0.019897461
- block_order: int32 [128], replicated, may hold values from 0 to 127, each once
Outputs:
- attended: bfloat16 [2, 9216, 16384], P(None, 'fsdp', 'tp')
- new_keys: bfloat16 [2, 9216, 1024], P(None, 'fsdp', 'tp')
Inputs may be any that keep to these rules, and one draw needn't show every extreme that they name: `lengths`: every row has at least two valid cached positions; some row holds 32. `block_order`: A permutation of the block rows.
All inputs are finite; a program needn't handle non-finite values.
Results may differ from a plain program's by a relative error of at most 0.0056.
Values may be sent and summed in bfloat16 or wider, within the bound.
A program may use at most 64 MiB of HBM per device.

v0:
```python
import math

import jax
import jax.numpy as jnp
from jax import lax
from jax.sharding import PartitionSpec as P

HD = 128
KVH = 8
QH = 128
BLK = 128


def per_device(
    hidden,
    queries,
    cache_keys,
    cache_values,
    new_values,
    lengths,
    base_weight,
    delta_values,
    delta_scales,
    block_order,
):
    columns = base_weight.shape[1]
    whole_rows = lax.all_gather(delta_values, "tp", axis=0, tiled=True)
    local_rows = lax.dynamic_slice_in_dim(whole_rows, lax.axis_index("tp") * columns, columns, 1)
    col_blocks = columns // BLK
    local_blocks = local_rows.shape[0] // BLK
    scaled = (
        local_rows.reshape(local_blocks, BLK, col_blocks, BLK).astype(jnp.float32)
        * delta_scales.astype(jnp.float32)[:, None, :, None]
    )
    pieces = scaled.reshape(local_blocks, BLK, columns).astype(jnp.bfloat16)
    gathered = lax.all_gather(pieces, "fsdp", axis=0, tiled=True)
    total_rows = gathered.shape[0]
    positions = jnp.arange(total_rows)
    inverse = jnp.sum(
        jnp.where(block_order[None, :] == positions[:, None], positions[None, :], 0), axis=1
    )
    ordered = jnp.take(gathered, inverse, axis=0)
    refreshed = (
        base_weight.astype(jnp.float32)
        + ordered.reshape(total_rows * BLK, columns).astype(jnp.float32)
    ).astype(jnp.bfloat16)
    steps_count, rows_count = (hidden.shape[0], hidden.shape[1])
    start_keys = jnp.zeros((steps_count, rows_count, columns), jnp.float32)
    piece = lax.all_gather(hidden, "tp", axis=2, tiled=True)
    width = piece.shape[2]
    product = jnp.dot(
        piece.reshape(steps_count * rows_count, width),
        refreshed,
        preferred_element_type=jnp.float32,
    )
    keys_sum = product.reshape(start_keys.shape)
    new_keys = keys_sum.astype(jnp.bfloat16)
    heads_here = columns // HD
    group = QH // KVH
    factor = 1.0 / math.sqrt(HD)
    capacity = cache_keys.shape[1]
    query = queries.reshape(steps_count, rows_count, heads_here, group, HD)
    ckeys = cache_keys.reshape(rows_count, capacity, heads_here, HD)
    cvals = cache_values.reshape(rows_count, capacity, heads_here, HD)
    nkeys = new_keys.reshape(steps_count, rows_count, heads_here, HD)
    nvals = new_values.reshape(steps_count, rows_count, heads_here, HD)
    cached = (
        jnp.einsum("srhgd,rchd->srhgc", query, ckeys, preferred_element_type=jnp.float32) * factor
    )
    fresh = (
        jnp.einsum("srhgd,urhd->srhgu", query, nkeys, preferred_element_type=jnp.float32) * factor
    )
    cache_mask = jnp.arange(capacity)[None, :] < lengths[:, None]
    step_mask = jnp.arange(steps_count)[None, :] <= jnp.arange(steps_count)[:, None]
    cached = jnp.where(cache_mask[None, :, None, None, :], cached, -1e30)
    fresh = jnp.where(step_mask[:, None, None, None, :], fresh, -1e30)
    joined = jnp.concatenate([cached, fresh], axis=4)
    top = jnp.max(joined, axis=4, keepdims=True)
    expo = jnp.exp(joined - top)
    weights = (expo / jnp.sum(expo, axis=4, keepdims=True)).astype(jnp.bfloat16)
    result = jnp.einsum(
        "srhgc,rchd->srhgd", weights[..., :capacity], cvals, preferred_element_type=jnp.float32
    )
    result = result + jnp.einsum(
        "srhgu,urhd->srhgd", weights[..., capacity:], nvals, preferred_element_type=jnp.float32
    )
    attended = result.reshape(steps_count, rows_count, heads_here * group * HD).astype(jnp.bfloat16)
    return (attended, new_keys)


def solution(mesh):
    in_specs = (
        P(None, "fsdp", "tp"),
        P(None, "fsdp", "tp"),
        P("fsdp", None, "tp"),
        P("fsdp", None, "tp"),
        P(None, "fsdp", "tp"),
        P("fsdp"),
        P(None, "tp"),
        P(("fsdp", "tp"), None),
        P("fsdp", "tp"),
        P(),
    )
    out_specs = (P(None, "fsdp", "tp"), P(None, "fsdp", "tp"))
    return jax.shard_map(
        per_device, mesh=mesh, in_specs=in_specs, out_specs=out_specs, check_vma=False
    )
```

profile of v0, /device:TPU:15, one launch (start us, length us, event | category | flops | bytes accessed | tf_op | source)
XLA Modules:
  0.0 279.9 jit_solution(1064776259275883131)
XLA Ops:
  7.2 0.0 copy-start
  7.2 0.0 copy-start.1
  7.2 0.0 copy-start.6
  7.2 0.0 copy-start.5
  7.2 0.0 copy-start.2
  7.2 0.0 all-gather.6.cloned.1.call-start
  7.3 15.1 %all_gather.9 = bf16[128,1024]{1,0:T(8,128)(2,1)S(1)} all-gather(bf16[16,1024]{1,0:T(8,128)(2,1)} %param.17), channel_id=1, replica_groups=mesh['fsdp'=128,'tp'=8] {'tp'}, dimensions={0}, use_global_device_ids=true | all-gather | bytes 294912 | tf_op jit(solution)/shard_map/all_gather | solution.py:27
  23.1 0.6 multiply_convert_fusion
  23.7 0.0 all-gather.6.cloned.1.call-update
  23.7 0.0 all-gather.4.cloned.1.call-start
  23.8 0.7 all-gather.4.cloned.1.call-update
  24.5 0.0 copy-done.1
  24.5 0.1 copy.45
  24.6 0.1 select_reduce_fusion
  24.8 0.1 iota_compare_fusion.1
  24.9 0.6 fusion.19
  25.5 0.1 broadcast_bitcast_fusion
  25.5 166.0 %all-gather.6.cloned.1.call-done = bf16[16384,128]{1,0:T(8,128)(2,1)} async-done(((bf16[128,128]{1,0:T(8,128)(2,1)}), bf16[16384,128]{1,0:T(8,128)(2,1)}) %all-gather.6.cloned.1.call-update) | async-done | bytes 4194320 | tf_op jit(solution)/shard_map/all_gather | solution.py:36
  191.6 5.3 %gather_fusion = bf16[128,128,128]{2,1,0:T(8,128)(2,1)} fusion(bf16[128,128,128]{2,1,0:T(8,128)(2,1)} %bitcast.79, s32[1024]{0:T(1024)S(1)} %pad_clamp_fusion), kind=kCustom, calls=%fused_computation | custom fusion | bytes 8389120 | tf_op jit(solution)/shard_map/jit(_take)/gather | solution.py:42
  196.9 11.5 %bitcast_select_fusion = bf16[16384,128]{1,0:T(8,128)(2,1)} fusion(bf16[128,128,128]{2,1,0:T(8,128)(2,1)} %gather_fusion, pred[16384]{0:T(1024)(128)(4,1)S(1)} %broadcast_bitcast_fusion), kind=kLoop, calls=%fused_computation.3 | loop fusion | flops 2097152 | bytes 8404992 | tf_op jit(solution)/shard_map/jit(_take)/select_n | solution.py:42
  208.4 53.0 %all-gather.4.cloned.1.call-done = bf16[2,72,16384]{2,1,0:T(8,128)(2,1)} async-done(((bf16[2,72,2048]{2,1,0:T(8,128)(2,1)}), bf16[2,72,16384]{2,1,0:T(8,128)(2,1)}) %all-gather.4.cloned.1.call-update) | async-done | bytes 4718608 | tf_op jit(solution)/shard_map/all_gather | solution.py:49
  261.4 6.4 %fusion.9 = bf16[128,144]{0,1:T(8,128)(2,1)S(1)} fusion(bf16[144,16384]{1,0:T(8,128)(2,1)} %bitcast.78, bf16[16384,128]{1,0:T(8,128)(2,1)} %bitcast_select_fusion, bf16[16384,128]{1,0:T(8,128)(2,1)} %param.16), kind=kOutput, calls=%fused_computation.17 | convolution fusion | flops 612386816 | bytes 13144064 | tf_op jit(solution)/shard_map/dot_general | solution.py:51
  267.8 0.0 copy-start.3
  267.8 0.6 fusion.20
  268.4 1.1 fusion.15
  269.6 1.1 divide_convert_fusion
  270.7 0.0 copy-start.4
  270.7 0.3 fusion.10
  271.0 0.5 copy-done.4
  271.5 0.4 fusion.7
  271.9 0.1 convert_element_type.73
  272.0 1.0 copy.34
  (10 shorter events, 0.1 us)
Async XLA Ops:
  7.2 263.6 %copy-start = (bf16[72,32,128]{2,1,0:T(8,128)(2,1)S(1)}, bf16[72,32,128]{2,1,0:T(8,128)(2,1)}, u32[]{:S(2)}) copy-start(bf16[72,32,128]{2,1,0:T(8,128)(2,1)} %param.13) | copy-start | bytes 1769476
  7.2 17.3 %copy-start.1 = (bf16[2,72,2048]{2,1,0:T(8,128)(2,1)S(1)}, bf16[2,72,2048]{2,1,0:T(8,128)(2,1)}, u32[]{:S(2)}) copy-start(bf16[2,72,2048]{2,1,0:T(8,128)(2,1)} %param.11) | copy-start | bytes 1769476
  7.2 17.4 %copy-start.6 = (s32[128]{0:T(128)S(1)}, s32[128]{0:T(128)}, u32[]{:S(2)}) copy-start(s32[128]{0:T(128)} %param.19) | copy-start | bytes 1540
  7.2 17.6 %copy-start.5 = (s32[72]{0:T(128)S(1)}, s32[72]{0:T(128)}, u32[]{:S(2)}) copy-start(s32[72]{0:T(128)} %param.15) | copy-start | bytes 868
  7.2 17.7 %copy-start.2 = (bf16[72,32,128]{2,1,0:T(8,128)(2,1)S(1)}, bf16[72,32,128]{2,1,0:T(8,128)(2,1)}, u32[]{:S(2)}) copy-start(bf16[72,32,128]{2,1,0:T(8,128)(2,1)} %param.12) | copy-start | bytes 1769476
  7.2 184.4 %all-gather.6.cloned.1.call-start = ((), (), s32[]{:S(2)}) async-start(), calls=%async_computation.1 | async-start | bytes 4227072 | tf_op jit(solution)/shard_map/all_gather | solution.py:36
  23.7 237.7 %all-gather.4.cloned.1.call-start = ((), (), s32[]{:S(2)}) async-start(), calls=%async_computation | async-start | bytes 5308416 | tf_op jit(solution)/shard_map/all_gather | solution.py:49
  267.8 1.8 copy-start.3
  270.7 0.8 copy-start.4
Sparse Core Ops, SparseCore 0:
  23.8 167.6 all-gather.5
  194.2 67.1 all-gather.3
where the time goes:
time: 280 us
  waiting for transfers between devices  220 us (79%)
  blocking collectives  15.1 us (5%)
  between operations  14.9 us (5%)
  other arithmetic  14.7 us (5%)
  matrix products  8.22 us (3%)
  local copies, waits for them, and re-layouts  7.11 us (3%)
    all_gather x1, waiting for transfers between devices, per_device(): gathered = lax.all_gather(pieces, 'fsdp', axis=0, tiled=True)  166 us
    all_gather x1, waiting for transfers between devices, per_device(): piece = lax.all_gather(hidden, 'tp', axis=2, tiled=True)  53 us
    all_gather x1, blocking collectives, per_device(): whole_rows = lax.all_gather(delta_values, 'tp', axis=0, tiled=True)  15.1 us
    select_n x2, other arithmetic, per_device(): ordered = jnp.take(gathered, inverse, axis=0)  11.5 us
    dot_general x1, matrix products, per_device(): jnp.dot(piece.reshape(steps_count * rows_count, width), refreshed, prefer...  6.36 us
  transfers between devices with their start and end apart: 2, of which 2 were waited for; matrix products, arithmetic and copies ran while one was open for 6% of the time, Pallas kernels for 0%

commit v1 on v0

v1 whole, which is shorter than its diff:
```python
import functools
import math

import jax
import jax.numpy as jnp
from jax import lax
from jax.experimental import pallas as pl
from jax.experimental.pallas import tpu as pltpu
from jax.sharding import PartitionSpec as P

HD = 128
TILE = 16
MESH = pl.DeviceIdType.MESH
F32 = jnp.float32
BF16 = jnp.bfloat16
GRID = {128: (8, 8, 2)}
NEG = -1e30


def contract(a, b, dims):
    return lax.dot_general(a, b, (dims, ((), ())), preferred_element_type=F32)


def kernel(
    dims,
    inverse_ref,
    lengths_ref,
    parcel_ref,
    delta_ref,
    hidden_hbm,
    queries_hbm,
    ckeys_hbm,
    cvals_hbm,
    nvals_ref,
    attended_ref,
    keys_ref,
    hidden_v,
    queries_v,
    ckeys_v,
    cvals_v,
    pick_v,
    regroup_v,
    hid_v,
    parcels_v,
    deltas_v,
    wide_v,
    *rest,
):
    nz, ny, nh, nt, rows = dims
    blocks = nz * ny * nh
    local_blocks = blocks // nt
    chips = nt // 2
    total = 2 * rows
    span = local_blocks * TILE
    width = nt * span
    heads = attended_ref.shape[2] // HD
    packs = rows // 8
    lines = 2 * heads * 8
    cap = ckeys_v.shape[1]
    keys8 = 8 * cap
    factor = 1.0 / math.sqrt(HD)

    w_v = rest[:chips]
    (
        partial_v,
        part_in_v,
        fresh_v,
        nval_v,
        q_v,
        o_v,
        m_v,
        l_v,
        mask_v,
        result_v,
        load_sem,
        p0_send,
        p0_recv,
        delta_send,
        delta_recv,
        hid_send,
        hid_recv,
        s1_send,
        s1_recv,
        s2_send,
        s2_recv,
        p6_send,
        p6_recv,
    ) = rest[chips:]

    f = lax.axis_index("fsdp")
    t = lax.axis_index("tp")
    h = lax.rem(f, nh)
    y = lax.rem(f // nh, ny)
    z = f // (nh * ny)

    def at(zz, yy, hh, tt):
        return ((zz * ny + yy) * nh + hh, tt)

    def y_peer(step):
        return at(z, lax.rem(y + step + ny, ny), h, t)

    def z_peer(step):
        return at(lax.rem(z + step + nz, nz), y, h, t)

    def x_peer(dh, d):
        return at(z, y, lax.rem(h + dh, nh), lax.rem(t + d, nt))

    x_peers = [(dh, d) for dh in range(nh) for d in range(nt) if (dh, d) != (0, 0)]

    loads = [
        pltpu.make_async_copy(src, dst, load_sem.at[i])
        for i, (src, dst) in enumerate(
            ((hidden_hbm, hidden_v), (queries_hbm, queries_v), (ckeys_hbm, ckeys_v), (cvals_hbm, cvals_v))
        )
    ]
    for load in loads:
        load.start()

    barrier = pltpu.get_barrier_semaphore()
    count = 0
    for peer in (
        [x_peer(*p) for p in x_peers]
        + [y_peer(s) for s in range(1, ny)]
        + [z_peer(s) for s in range(1, nz)]
    ):
        pl.semaphore_signal(barrier, inc=1, device_id=peer, device_id_type=MESH)
        count += 1
    pl.semaphore_wait(barrier, count)

    def remote(src, dst, send, recv, peer):
        return pltpu.make_async_remote_copy(
            src_ref=src, dst_ref=dst, send_sem=send, recv_sem=recv, device_id=peer, device_id_type=MESH
        )

    sent = []

    def start(copy):
        copy.start()
        sent.append(copy)

    for i, (dh, d) in enumerate(x_peers):
        start(
            remote(
                parcel_ref.at[lax.rem(t + d, nt)],
                parcels_v.at[h * nt + t],
                p0_send.at[i],
                p0_recv.at[i],
                x_peer(dh, d),
            )
        )
    if nh > 1:
        start(remote(delta_ref, deltas_v.at[h], delta_send, delta_recv, x_peer(1, 0)))
    parcels_v[h * nt + t] = parcel_ref[t]
    deltas_v[h] = delta_ref[...]

    lane_k = lax.broadcasted_iota(jnp.int32, (width, span), 0)
    lane_l = lax.broadcasted_iota(jnp.int32, (width, span), 1)
    target = (lane_k // (nt * TILE)) * TILE + lax.rem(lane_k, TILE)
    pick_v[...] = jnp.where(target == lane_l, 1.0, 0.0).astype(BF16)
    loads[0].wait()
    group_of = lax.rem(lax.broadcasted_iota(jnp.int32, (rows, width), 1) // TILE, nt)

    def regroup(g, carry):
        halves = []
        for s in range(2):
            chosen = jnp.where(group_of == g, hidden_v[s].astype(F32), 0.0).astype(BF16)
            halves.append(contract(chosen, pick_v[...], ((1,), (0,))))
        regroup_v[g] = jnp.concatenate(halves, axis=0).astype(BF16)
        return carry

    lax.fori_loop(0, nt, regroup, 0)
    for d in range(1, nt):
        start(
            remote(
                regroup_v.at[lax.rem(t + d, nt)],
                hid_v.at[t],
                hid_send.at[d],
                hid_recv.at[d],
                x_peer(0, d),
            )
        )
    hid_v[t] = regroup_v[t]

    for i, (dh, d) in enumerate(x_peers):
        source = lax.rem(h + nh - dh, nh) * nt + lax.rem(t + nt - d, nt)
        remote(parcel_ref.at[0], parcels_v.at[source], p0_send.at[i], p0_recv.at[i], x_peer(dh, d)).wait_recv()
    if nh > 1:
        remote(delta_ref, deltas_v.at[1 - h], delta_send, delta_recv, x_peer(1, 0)).wait_recv()

    def axes(c):
        if c < (chips + 1) // 2:
            return (y, ny, y_peer), (z, nz, z_peer)
        return (z, nz, z_peer), (y, ny, y_peer)

    for c in range(chips):
        (a, na, _), (b, nb, _) = axes(c)
        own = (b * na + a) * nh
        for hh in range(nh):
            cols = []
            for k in range(2):
                col = 2 * c + k
                parcel = parcels_v[hh * nt + col].astype(F32)
                scaled = deltas_v[hh, :, col * HD : (col + 1) * HD].astype(F32) * parcel[TILE:]
                scaled = scaled.astype(BF16).astype(F32)
                cols.append(parcel[:TILE] + scaled)
            w_v[c][own + hh] = jnp.concatenate(cols, axis=1).astype(BF16)

    order = []
    for i in range((chips + 1) // 2):
        pair = [i, chips - 1 - i]
        order.append(pair if pair[0] != pair[1] else pair[:1])

    def stage1_piece(c, source_a):
        (a, na, _), (b, nb, _) = axes(c)
        return w_v[c].at[pl.ds((b * na + source_a) * nh, nh)]

    def stage1_send(c):
        (a, na, peer), _ = axes(c)
        for s in range(1, na):
            start(remote(stage1_piece(c, a), stage1_piece(c, a), s1_send.at[c, s], s1_recv.at[c, s], peer(s)))

    def stage1_wait(c):
        (a, na, peer), _ = axes(c)
        for s in range(1, na):
            piece = stage1_piece(c, lax.rem(a + na - s, na))
            remote(piece, piece, s1_send.at[c, s], s1_recv.at[c, s], peer(s)).wait_recv()

    def unit(c, which, half):
        (a, na, _), (b, nb, _) = axes(c)
        size = na * nh // 2
        start_row = lax.rem(b + which + 2 * nb, nb) * (na * nh) + half * size
        return w_v[c].at[pl.ds(start_row, size)]

    def hops(c, way):
        nb = axes(c)[1][1]
        return nb // 2 if way == 0 else nb - 1 - nb // 2

    def sign(group, way):
        return 1 if (group + way) % 2 == 0 else -1

    def stage2_send(group, step, half):
        for c in order[group]:
            peer = axes(c)[1][2]
            for way in range(2):
                if step < hops(c, way):
                    sg = sign(group, way)
                    piece = unit(c, -sg * step, half)
                    start(
                        remote(
                            piece, piece, s2_send.at[c, way, step, half], s2_recv.at[c, way, step, half], peer(sg)
                        )
                    )

    def stage2_wait(group, step, half):
        for c in order[group]:
            peer = axes(c)[1][2]
            for way in range(2):
                if step < hops(c, way):
                    sg = sign(group, way)
                    piece = unit(c, -sg * (step + 1), half)
                    remote(
                        piece, piece, s2_send.at[c, way, step, half], s2_recv.at[c, way, step, half], peer(sg)
                    ).wait_recv()

    for pair in order:
        for c in pair:
            stage1_send(c)

    for load in loads[1:]:
        load.wait()
    wide_v[...] = queries_v[...].astype(F32)
    line = lax.broadcasted_iota(jnp.int32, (lines, keys8), 0)
    place = lax.broadcasted_iota(jnp.int32, (lines, keys8), 1)
    mask_v[...] = jnp.where(lax.rem(line, 8) == place // cap, 0.0, NEG)
    nval_v[...] = jnp.concatenate([nvals_ref[0].astype(F32), nvals_ref[1].astype(F32)], axis=0)

    def cached(i, carry):
        row = pl.multiple_of(i * 8, 8)
        parts = [
            wide_v[s, pl.ds(row, 8), g * HD : (g + 1) * HD] for s in range(2) for g in range(heads)
        ]
        q = jnp.concatenate(parts, axis=0).astype(BF16)
        q_v[i] = q
        k = ckeys_v[pl.ds(row, 8)].reshape(keys8, HD)
        v = cvals_v[pl.ds(row, 8)].reshape(keys8, HD)
        slot = lax.broadcasted_iota(jnp.int32, (1, keys8), 1)
        limit = jnp.zeros((1, keys8), jnp.int32)
        for r in range(8):
            limit = jnp.where(slot // cap == r, lengths_ref[row + r], limit)
        open_slot = lax.rem(slot, cap) < limit
        scores = contract(q, k, ((1,), (1,))) * factor
        scores = jnp.where(open_slot, scores + mask_v[...], NEG)
        top = jnp.max(scores, axis=1, keepdims=True)
        expo = jnp.exp(scores - top)
        o_v[i] = contract(expo.astype(BF16), v, ((1,), (0,)))
        m_v[i] = jnp.broadcast_to(top, (lines, HD))
        l_v[i] = jnp.broadcast_to(jnp.sum(expo, axis=1, keepdims=True), (lines, HD))
        return carry

    done = [0]

    def some_cached(upto):
        upto = min(upto, packs)
        if upto > done[0]:
            lax.fori_loop(done[0], upto, cached, 0)
            done[0] = upto

    def product(c):
        total_ = jnp.zeros((total, 2 * HD), F32)
        (_, na, _), (_, nb, _) = axes(c)
        kind = 0 if c < (chips + 1) // 2 else 1

        def step(k, acc):
            tiles = [w_v[c][inverse_ref[kind, k * local_blocks + j]] for j in range(local_blocks)]
            w = jnp.concatenate(tiles, axis=0)
            return acc + contract(hid_v[k], w, ((1,), (0,)))

        acc = lax.fori_loop(0, nt, step, total_)
        for k in range(2):
            owner = 2 * c + k
            partial_v[owner] = acc[:, k * HD : (k + 1) * HD]

            @pl.when(t != owner)
            def _():
                remote(
                    partial_v.at[owner],
                    part_in_v.at[t],
                    p6_send.at[owner],
                    p6_recv.at[lax.rem(owner - t + nt, nt)],
                    (f, owner),
                ).start()

    groups = len(order)
    steps = max(hops(c, 0) for c in range(chips))
    pending = []
    waited_hidden = False
    for group in range(groups):
        for c in order[group]:
            stage1_wait(c)
        for half in range(2):
            stage2_send(group, 0, half)
        if group > 0:
            for half in range(2):
                stage2_wait(group - 1, steps - 1, half)
            pending += order[group - 1]
        for step in range(1, steps):
            for half in range(2):
                if group == 0:
                    some_cached(-(-packs * (2 * step + half - 1) // max(1, 2 * (steps - 1))))
                stage2_wait(group, step - 1, half)
                stage2_send(group, step, half)
                if pending:
                    if not waited_hidden:
                        waited_hidden = True
                        for d in range(1, nt):
                            remote(
                                regroup_v.at[0],
                                hid_v.at[lax.rem(t + nt - d, nt)],
                                hid_send.at[d],
                                hid_recv.at[d],
                                x_peer(0, d),
                            ).wait_recv()
                    product(pending.pop(0))
    some_cached(packs)
    for half in range(2):
        stage2_wait(groups - 1, steps - 1, half)
    pending += order[groups - 1]
    if not waited_hidden:
        for d in range(1, nt):
            remote(
                regroup_v.at[0], hid_v.at[lax.rem(t + nt - d, nt)], hid_send.at[d], hid_recv.at[d], x_peer(0, d)
            ).wait_recv()
    for c in pending:
        product(c)

    for d in range(1, nt):
        remote(
            partial_v.at[0], part_in_v.at[lax.rem(t + nt - d, nt)], p6_send.at[0], p6_recv.at[d], x_peer(0, d)
        ).wait_recv()
    keys = partial_v[t]
    for d in range(1, nt):
        keys = keys + part_in_v[lax.rem(t + nt - d, nt)]
    keys16 = keys.astype(BF16)
    keys32 = keys16.astype(F32)
    fresh_v[...] = keys32
    keys_ref[0] = keys32[:rows].astype(BF16)
    keys_ref[1] = keys32[rows:].astype(BF16)

    line2 = lax.broadcasted_iota(jnp.int32, (lines, 16), 0)
    place2 = lax.broadcasted_iota(jnp.int32, (lines, 16), 1)
    allowed = (lax.rem(line2, 8) == lax.rem(place2, 8)) & (place2 // 8 <= line2 // (heads * 8))

    def finish(i, carry):
        row = pl.multiple_of(i * 8, 8)
        late = pl.multiple_of(rows + i * 8, 8)
        nk = jnp.concatenate([fresh_v[pl.ds(row, 8)], fresh_v[pl.ds(late, 8)]], axis=0).astype(BF16)
        nv = jnp.concatenate([nval_v[pl.ds(row, 8)], nval_v[pl.ds(late, 8)]], axis=0).astype(BF16)
        scores = jnp.where(allowed, contract(q_v[i], nk, ((1,), (1,))) * factor, NEG)
        old = m_v[i]
        top = jnp.maximum(old, jnp.max(scores, axis=1, keepdims=True))
        keep = jnp.exp(old - top)
        expo = jnp.exp(scores - top[:, :16])
        weight = l_v[i] * keep + jnp.sum(expo, axis=1, keepdims=True)
        out = (o_v[i] * keep + contract(expo.astype(BF16), nv, ((1,), (0,)))) / weight
        for s in range(2):
            for g in range(heads):
                at_line = (s * heads + g) * 8
                result_v[s, pl.ds(row, 8), g * HD : (g + 1) * HD] = out[at_line : at_line + 8]
        return carry

    lax.fori_loop(0, packs, finish, 0)
    attended_ref[...] = result_v[...].astype(BF16)

    for copy in sent:
        copy.wait_send()
    for owner in range(nt):

        @pl.when(t != owner)
        def _():
            remote(
                partial_v.at[owner], part_in_v.at[t], p6_send.at[owner], p6_recv.at[0], (f, owner)
            ).wait_send()


def per_device(
    grid,
    nt,
    hidden,
    queries,
    cache_keys,
    cache_values,
    new_values,
    lengths,
    base_weight,
    delta_values,
    delta_scales,
    block_order,
):
    nz, ny, nh = grid
    blocks = nz * ny * nh
    rows = hidden.shape[1]
    blk = base_weight.shape[0] // blocks
    assert blk == nt * TILE and base_weight.shape[1] == HD
    f = lax.axis_index("fsdp")
    block = lax.dynamic_slice_in_dim(base_weight, block_order[f] * blk, blk, 0)
    scale = jnp.broadcast_to(delta_scales.reshape(1, 1, 1), (nt, TILE, HD))
    parcel = jnp.concatenate([block.reshape(nt, TILE, HD), scale], axis=1)
    numbers = jnp.arange(blocks, dtype=jnp.int32)
    zz, yy, hh = numbers // (ny * nh), (numbers // nh) % ny, numbers % nh
    slots = jnp.stack([numbers, (yy * nz + zz) * nh + hh])
    inverse = jnp.sum(
        jnp.where(block_order[None, None, :] == numbers[None, :, None], slots[:, None, :], 0), axis=2
    ).astype(jnp.int32)

    chips = nt // 2
    total = 2 * rows
    span = blocks // nt * TILE
    width = nt * span
    heads = queries.shape[2] // HD
    packs = rows // 8
    lines = 2 * heads * 8
    cap = cache_keys.shape[1]
    ring = max(ny, nz)
    xs = nh * nt - 1
    dma = pltpu.SemaphoreType.DMA
    scratch = [
        pltpu.VMEM(hidden.shape, BF16),
        pltpu.VMEM(queries.shape, BF16),
        pltpu.VMEM(cache_keys.shape, BF16),
        pltpu.VMEM(cache_values.shape, BF16),
        pltpu.VMEM((width, span), BF16),
        pltpu.VMEM((nt, total, span), BF16),
        pltpu.VMEM((nt, total, span), BF16),
        pltpu.VMEM((nh * nt, 2 * TILE, HD), BF16),
        pltpu.VMEM((nh, TILE, nt * HD), BF16),
        pltpu.VMEM(queries.shape, F32),
        *[pltpu.VMEM((blocks, TILE, 2 * HD), BF16) for _ in range(chips)],
        pltpu.VMEM((nt, total, HD), F32),
        pltpu.VMEM((nt, total, HD), F32),
        pltpu.VMEM((total, HD), F32),
        pltpu.VMEM((total, HD), F32),
        pltpu.VMEM((packs, lines, HD), BF16),
        pltpu.VMEM((packs, lines, HD), F32),
        pltpu.VMEM((packs, lines, HD), F32),
        pltpu.VMEM((packs, lines, HD), F32),
        pltpu.VMEM((lines, 8 * cap), F32),
        pltpu.VMEM(queries.shape, F32),
        dma((4,)),
        dma((xs,)),
        dma((xs,)),
        dma,
        dma,
        dma((nt,)),
        dma((nt,)),
        dma((chips, ring)),
        dma((chips, ring)),
        dma((chips, 2, ring // 2, 2)),
        dma((chips, 2, ring // 2, 2)),
        dma((nt,)),
        dma((nt,)),
    ]
    vmem = pl.BlockSpec(memory_space=pltpu.VMEM)
    smem = pl.BlockSpec(memory_space=pltpu.SMEM)
    hbm = pl.BlockSpec(memory_space=pl.ANY)
    return tuple(
        pl.pallas_call(
            functools.partial(kernel, (nz, ny, nh, nt, rows)),
            out_shape=(
                jax.ShapeDtypeStruct(queries.shape, BF16),
                jax.ShapeDtypeStruct((2, rows, HD), BF16),
            ),
            in_specs=[smem, smem, vmem, vmem, hbm, hbm, hbm, hbm, vmem],
            out_specs=(vmem, vmem),
            scratch_shapes=scratch,
            compiler_params=pltpu.CompilerParams(
                collective_id=0, has_side_effects=True, vmem_limit_bytes=50 * 2**20
            ),
            name="refresh_project_attend",
        )(inverse, lengths, parcel, delta_values, hidden, queries, cache_keys, cache_values, new_values)
    )


def solution(mesh, grid=None):
    grid = grid or GRID[mesh.shape["fsdp"]]
    in_specs = (
        P(None, "fsdp", "tp"),
        P(None, "fsdp", "tp"),
        P("fsdp", None, "tp"),
        P("fsdp", None, "tp"),
        P(None, "fsdp", "tp"),
        P("fsdp"),
        P(None, "tp"),
        P(("fsdp", "tp"), None),
        P("fsdp", "tp"),
        P(),
    )
    out_specs = (P(None, "fsdp", "tp"), P(None, "fsdp", "tp"))
    return jax.shard_map(
        functools.partial(per_device, grid, mesh.shape["tp"]),
        mesh=mesh,
        in_specs=in_specs,
        out_specs=out_specs,
        check_vma=False,
    )
```

time: 280 us -> 97.9 us (0.35)
  the two profiles are of different devices: /device:TPU:15 before, /device:TPU:13 now
where the time goes in v1:
time: 97.9 us; the launch traced here: 97.3 us
  Pallas kernels  84.6 us (86%)
  local copies, waits for them, and re-layouts  9.89 us (10%)
  between operations  1.99 us (2%)
    pallas_call x1, Pallas kernels, per_device(): pl.pallas_call(functools.partial(kernel, (nz, ny, nh, nt, rows)), out_sha...  84.6 us
    unnamed x16, local copies, waits for them, and re-layouts  7.86 us
    dynamic_slice x2, local copies, waits for them, and re-layouts, per_device(): block = lax.dynamic_slice_in_dim(base_weight, block_order[f] * blk, blk, 0)  2.01 us

profile of v1, /device:TPU:13, one launch (start us, length us, event | category | flops | bytes accessed | tf_op | source)
XLA Modules:
  0.0 97.3 jit_solution(14554212847639124409)
XLA Ops:
  1.3 1.2 %dynamic_slice.6 = s32[1]{0:T(128)} dynamic-slice(s32[128]{0:T(128)} %param.19, s32[]{:T(128)S(6)} %select_n.62), dynamic_slice_sizes={1} | dynamic-slice | bytes 12 | tf_op jit(solution)/shard_map/dynamic_slice | solution.py:445
  3.2 0.7 iota_compare_fusion
  3.9 0.1 select_reduce_fusion.inverse_ref
  4.0 0.8 constant_dynamic-slice_fusion
  4.8 0.0 copy-start
  4.8 1.1 %copy-done = bf16[2,72,2048]{2,1,0:T(8,128)(2,1)S(1)} copy-done((bf16[2,72,2048]{2,1,0:T(8,128)(2,1)S(1)}, bf16[2,72,2048]{2,1,0:T(8,128)(2,1)}, u32[]{:S(2)}) %copy-start) | copy-done | bytes 589848
  5.9 0.0 copy-start.1
  5.9 1.1 %copy-done.1 = bf16[2,72,2048]{2,1,0:T(8,128)(2,1)S(1)} copy-done((bf16[2,72,2048]{2,1,0:T(8,128)(2,1)S(1)}, bf16[2,72,2048]{2,1,0:T(8,128)(2,1)}, u32[]{:S(2)}) %copy-start.1) | copy-done | bytes 589848
  6.9 0.0 copy-start.2
  6.9 1.1 %copy-done.2 = bf16[72,32,128]{2,1,0:T(8,128)(2,1)S(1)} copy-done((bf16[72,32,128]{2,1,0:T(8,128)(2,1)S(1)}, bf16[72,32,128]{2,1,0:T(8,128)(2,1)}, u32[]{:S(2)}) %copy-start.2) | copy-done | bytes 589848
  8.0 0.0 copy-start.3
  8.0 1.1 %copy-done.3 = bf16[72,32,128]{2,1,0:T(8,128)(2,1)S(1)} copy-done((bf16[72,32,128]{2,1,0:T(8,128)(2,1)S(1)}, bf16[72,32,128]{2,1,0:T(8,128)(2,1)}, u32[]{:S(2)}) %copy-start.3) | copy-done | bytes 589848
  9.1 0.0 copy-start.4
  9.1 0.8 copy-done.4
  9.8 0.0 copy-start.5
  9.8 0.8 copy-done.5
  10.6 0.0 copy-start.6
  10.6 0.7 copy-done.6
  11.2 84.6 %refresh_project_attend.1 = (bf16[2,72,2048]{2,1,0:T(8,128)(2,1)S(1)}, bf16[2,72,128]{2,1,0:T(8,128)(2,1)S(1)}) custom-call(s32[2,128]{1,0:T(2,128)S(1)} %select_reduce_fusion.inverse_ref, s32[72]{0:T(128)S(1)} %copy-done.6, bf16[8,32,128]{2,1,0:T(8,128)(2,1)S(1)} %concatenate.3.parcel_ref, bf16[16,1024]{1,0:T(8,128)(2,1)S(1)} %copy-done.5, ...), custom_call_target="tpu_custom_call" | custom-call | tf_op jit(solution)/shard_map/refresh_project_attend/pallas_call | solution.py:506
  95.9 0.8 copy.15
  96.7 0.6 copy.16
  (4 shorter events, 0.0 us)
Async XLA Ops:
  4.8 1.1 %copy-start = (bf16[2,72,2048]{2,1,0:T(8,128)(2,1)S(1)}, bf16[2,72,2048]{2,1,0:T(8,128)(2,1)}, u32[]{:S(2)}) copy-start(bf16[2,72,2048]{2,1,0:T(8,128)(2,1)} %hidden_hbm.1) | copy-start | bytes 1769476
  5.9 1.1 %copy-start.1 = (bf16[2,72,2048]{2,1,0:T(8,128)(2,1)S(1)}, bf16[2,72,2048]{2,1,0:T(8,128)(2,1)}, u32[]{:S(2)}) copy-start(bf16[2,72,2048]{2,1,0:T(8,128)(2,1)} %queries_hbm.1) | copy-start | bytes 1769476
  6.9 1.1 %copy-start.2 = (bf16[72,32,128]{2,1,0:T(8,128)(2,1)S(1)}, bf16[72,32,128]{2,1,0:T(8,128)(2,1)}, u32[]{:S(2)}) copy-start(bf16[72,32,128]{2,1,0:T(8,128)(2,1)} %ckeys_hbm.1) | copy-start | bytes 1769476
  8.0 1.1 %copy-start.3 = (bf16[72,32,128]{2,1,0:T(8,128)(2,1)S(1)}, bf16[72,32,128]{2,1,0:T(8,128)(2,1)}, u32[]{:S(2)}) copy-start(bf16[72,32,128]{2,1,0:T(8,128)(2,1)} %cvals_hbm.1) | copy-start | bytes 1769476
  9.1 0.8 copy-start.4
  9.8 0.8 copy-start.5
  10.6 0.7 copy-start.6

commit v2 on v1

v2 whole, which is shorter than its diff:
```python
import functools
import math

import jax
import jax.numpy as jnp
from jax import lax
from jax.experimental import pallas as pl
from jax.experimental.pallas import tpu as pltpu
from jax.sharding import PartitionSpec as P

HD = 128
TILE = 16
MESH = pl.DeviceIdType.MESH
F32 = jnp.float32
BF16 = jnp.bfloat16
GRID = {128: (8, 8, 2)}
NEG = -1e30
CUTS = 2


def contract(a, b, dims):
    return lax.dot_general(a, b, (dims, ((), ())), preferred_element_type=F32)


def kernel(
    dims,
    order_hbm,
    lengths_hbm,
    scale_hbm,
    base_hbm,
    delta_hbm,
    hidden_hbm,
    queries_hbm,
    ckeys_hbm,
    cvals_hbm,
    nvals_hbm,
    attended_ref,
    keys_ref,
    order_ref,
    lengths_ref,
    target_v,
    scale_v,
    base_v,
    delta_ref,
    nvals_ref,
    parcel_ref,
    hidden_v,
    queries_v,
    ckeys_v,
    cvals_v,
    hidden_all_v,
    pick_v,
    regroup_v,
    hid_v,
    parcels_v,
    deltas_v,
    wide_v,
    *rest,
):
    nz, ny, nh, nt, rows = dims
    blocks = nz * ny * nh
    local_blocks = blocks // nt
    chips = nt // 2
    total = 2 * rows
    sub = TILE // nh
    span = local_blocks * sub
    width = nt * nh * span
    heads = attended_ref.shape[2] // HD
    packs = rows // 8
    lines = 2 * heads * 8
    cap = ckeys_v.shape[1]
    keys8 = 8 * cap
    factor = 1.0 / math.sqrt(HD)

    bands = 2
    band_chips = chips // bands
    w_v = rest[:bands]
    (
        ordered_v,
        mine_v,
        give_v,
        take_v,
        out_v,
        part_in_v,
        fresh_v,
        nval_v,
        q_v,
        o_v,
        m_v,
        l_v,
        mask_v,
        result_v,
        load_sem,
        p0_send,
        p0_recv,
        delta_send,
        delta_recv,
        hid_send,
        hid_recv,
        s1_send,
        s1_recv,
        s2_send,
        s2_recv,
        pair_send,
        pair_recv,
        p6_send,
        p6_recv,
    ) = rest[bands:]

    f = lax.axis_index("fsdp")
    t = lax.axis_index("tp")
    h = lax.rem(f, nh)
    y = lax.rem(f // nh, ny)
    z = f // (nh * ny)

    def at(zz, yy, hh, tt):
        return ((zz * ny + yy) * nh + hh, tt)

    def y_peer(step):
        return at(z, lax.rem(y + step + ny, ny), h, t)

    def z_peer(step):
        return at(lax.rem(z + step + nz, nz), y, h, t)

    def x_peer(dh, d):
        return at(z, y, lax.rem(h + dh, nh), lax.rem(t + d, nt))

    x_peers = [(dh, d) for dh in range(nh) for d in range(nt) if (dh, d) != (0, 0)]

    loads = [
        pltpu.make_async_copy(src, dst, load_sem.at[i])
        for i, (src, dst) in enumerate(
            (
                (order_hbm, order_ref),
                (scale_hbm, scale_v),
                (base_hbm, base_v),
                (delta_hbm, delta_ref),
                (hidden_hbm, hidden_v),
                (lengths_hbm, lengths_ref),
                (queries_hbm, queries_v),
                (ckeys_hbm, ckeys_v),
                (cvals_hbm, cvals_v),
                (nvals_hbm, nvals_ref),
            )
        )
    ]
    for load in loads:
        load.start()

    barrier = pltpu.get_barrier_semaphore()
    count = 0
    for peer in (
        [x_peer(*p) for p in x_peers]
        + [y_peer(s) for s in range(1, ny)]
        + [z_peer(s) for s in range(1, nz)]
    ):
        pl.semaphore_signal(barrier, inc=1, device_id=peer, device_id_type=MESH)
        count += 1
    for load in loads[:4]:
        load.wait()
    parcel_ref[:, :TILE] = base_v[order_ref[f]].reshape(nt, TILE, HD)
    parcel_ref[:, TILE:] = jnp.broadcast_to(scale_v[...].reshape(1, 1, 1), (nt, TILE, HD))
    pl.semaphore_wait(barrier, count)

    def remote(src, dst, send, recv, peer):
        return pltpu.make_async_remote_copy(
            src_ref=src, dst_ref=dst, send_sem=send, recv_sem=recv, device_id=peer, device_id_type=MESH
        )

    sent = []

    def start(copy):
        copy.start()
        sent.append(copy)

    for i, (dh, d) in enumerate(x_peers):
        start(
            remote(
                parcel_ref.at[lax.rem(t + d, nt)],
                parcels_v.at[h * nt + t],
                p0_send.at[i],
                p0_recv.at[i],
                x_peer(dh, d),
            )
        )
    if nh > 1:
        start(remote(delta_ref, deltas_v.at[h], delta_send, delta_recv, x_peer(1, 0)))
    parcels_v[h * nt + t] = parcel_ref[t]
    deltas_v[h] = delta_ref[...]

    lane_k = lax.broadcasted_iota(jnp.int32, (width, nh * span), 0)
    lane_l = lax.broadcasted_iota(jnp.int32, (width, nh * span), 1)
    target = lax.rem(lane_k, TILE) // sub * span + lane_k // (nt * TILE) * sub + lax.rem(lane_k, sub)
    pick_v[...] = jnp.where(target == lane_l, 1.0, 0.0).astype(BF16)
    loads[4].wait()
    hidden_all_v[...] = jnp.concatenate([hidden_v[0].astype(F32), hidden_v[1].astype(F32)], axis=0).astype(BF16)
    group_of = lax.rem(lax.broadcasted_iota(jnp.int32, (1, width), 1) // TILE, nt)

    def regroup(g, carry):
        chosen = hidden_all_v[...] * jnp.where(group_of == g, 1.0, 0.0).astype(BF16)
        out = contract(chosen, pick_v[...], ((1,), (0,))).astype(BF16)
        for hh in range(nh):
            regroup_v[hh * nt + g] = out[:, hh * span : (hh + 1) * span]
        return carry

    lax.fori_loop(0, nt, regroup, 0)
    for i, (dh, d) in enumerate(x_peers):
        start(
            remote(
                regroup_v.at[lax.rem(h + dh, nh) * nt + lax.rem(t + d, nt)],
                hid_v.at[h * nt + t],
                hid_send.at[i],
                hid_recv.at[i],
                x_peer(dh, d),
            )
        )
    hid_v[h * nt + t] = regroup_v[h * nt + t]

    def hidden_wait():
        for i, (dh, d) in enumerate(x_peers):
            source = lax.rem(h + nh - dh, nh) * nt + lax.rem(t + nt - d, nt)
            remote(regroup_v.at[0], hid_v.at[source], hid_send.at[i], hid_recv.at[i], x_peer(dh, d)).wait_recv()

    for i, (dh, d) in enumerate(x_peers):
        source = lax.rem(h + nh - dh, nh) * nt + lax.rem(t + nt - d, nt)
        remote(parcel_ref.at[0], parcels_v.at[source], p0_send.at[i], p0_recv.at[i], x_peer(dh, d)).wait_recv()
    if nh > 1:
        remote(delta_ref, deltas_v.at[1 - h], delta_send, delta_recv, x_peer(1, 0)).wait_recv()

    def axes(c):
        if c == 0:
            return (y, ny, y_peer), (z, nz, z_peer)
        return (z, nz, z_peer), (y, ny, y_peer)

    def half_of(rows16):
        out = rows16[:sub]
        for hh in range(1, nh):
            out = jnp.where(h == hh, rows16[hh * sub : (hh + 1) * sub], out)
        return out

    for c in range(bands):
        (a, na, _), (b, nb, _) = axes(c)
        cols = []
        for col in range(c * nt // bands, (c + 1) * nt // bands):
            parts = []
            for hh in range(nh):
                parcel = parcels_v[hh * nt + col].astype(F32)
                update = deltas_v[hh, :, col * HD : (col + 1) * HD].astype(F32)
                scaled = (half_of(update) * parcel[TILE : TILE + sub]).astype(BF16).astype(F32)
                parts.append(half_of(parcel[:TILE]) + scaled)
            cols.append(jnp.concatenate(parts, axis=0))
        w_v[c][b * na + a] = jnp.concatenate(cols, axis=1).astype(BF16)

    def stage1_piece(c, source_a):
        (a, na, _), (b, nb, _) = axes(c)
        return w_v[c].at[pl.ds(b * na + source_a, 1)]

    def stage1_send(c):
        (a, na, peer), _ = axes(c)
        for s in range(1, na):
            start(remote(stage1_piece(c, a), stage1_piece(c, a), s1_send.at[c, s], s1_recv.at[c, s], peer(s)))

    def stage1_wait(c):
        (a, na, peer), _ = axes(c)
        for s in range(1, na):
            piece = stage1_piece(c, lax.rem(a + na - s, na))
            remote(piece, piece, s1_send.at[c, s], s1_recv.at[c, s], peer(s)).wait_recv()

    def unit(c, which, half):
        (a, na, _), (b, nb, _) = axes(c)
        size = na // CUTS
        start_row = lax.rem(b + which + 2 * nb, nb) * na + half * size
        return w_v[c].at[pl.ds(start_row, size)]

    def hops(c, way, half):
        nb = axes(c)[1][1]
        return nb // 2 if (half < CUTS // 2) == (way == 0) else nb - 1 - nb // 2

    def stage2_each(step, half, ahead, act):
        for c in range(bands):
            peer = axes(c)[1][2]
            for way, sign in enumerate((1, -1)):
                if step < hops(c, way, half):
                    piece = unit(c, -sign * (step + ahead), half)
                    act(
                        remote(
                            piece, piece, s2_send.at[c, way, step, half], s2_recv.at[c, way, step, half], peer(sign)
                        )
                    )

    def stage2_send(step, half):
        stage2_each(step, half, 0, start)

    def stage2_wait(step, half):
        stage2_each(step, half, 1, lambda copy: copy.wait_recv())

    for c in range(bands):
        stage1_send(c)

    for load in loads[5:]:
        load.wait()
    wide_v[...] = queries_v[...].astype(F32)
    line = lax.broadcasted_iota(jnp.int32, (lines, keys8), 0)
    place = lax.broadcasted_iota(jnp.int32, (lines, keys8), 1)
    mask_v[...] = jnp.where(lax.rem(line, 8) == place // cap, 0.0, NEG)
    nval_v[...] = jnp.concatenate([nvals_ref[0].astype(F32), nvals_ref[1].astype(F32)], axis=0)

    place_l = lax.broadcasted_iota(jnp.int32, (1, blocks * sub), 1)

    def aim(p, row):
        return jnp.where(place_l // sub == p, order_ref[p] * sub, row)

    aimed = lax.fori_loop(0, blocks, aim, jnp.zeros((1, blocks * sub), jnp.int32))
    target_v[...] = aimed + lax.rem(place_l, sub)

    def cached(i, carry):
        row = pl.multiple_of(i * 8, 8)
        parts = [
            wide_v[s, pl.ds(row, 8), g * HD : (g + 1) * HD] for s in range(2) for g in range(heads)
        ]
        q = jnp.concatenate(parts, axis=0).astype(BF16)
        q_v[i] = q
        k = ckeys_v[pl.ds(row, 8)].reshape(keys8, HD)
        v = cvals_v[pl.ds(row, 8)].reshape(keys8, HD)
        slot = lax.broadcasted_iota(jnp.int32, (1, keys8), 1)
        limit = jnp.zeros((1, keys8), jnp.int32)
        for r in range(8):
            limit = jnp.where(slot // cap == r, lengths_ref[row + r], limit)
        open_slot = lax.rem(slot, cap) < limit
        scores = contract(q, k, ((1,), (1,))) * factor
        scores = jnp.where(open_slot, scores + mask_v[...], NEG)
        top = jnp.max(scores, axis=1, keepdims=True)
        expo = jnp.exp(scores - top)
        o_v[i] = contract(expo.astype(BF16), v, ((1,), (0,)))
        m_v[i] = jnp.broadcast_to(top, (lines, HD))
        l_v[i] = jnp.broadcast_to(jnp.sum(expo, axis=1, keepdims=True), (lines, HD))
        return carry

    done = [0]

    def some_cached(upto):
        upto = min(upto, packs)
        if upto > done[0]:
            lax.fori_loop(done[0], upto, cached, 0)
            done[0] = upto

    def reorder():
        lanes = [
            jnp.concatenate([hid_v[hh * nt + k] for k in range(nt)], axis=1) for hh in range(nh)
        ]
        natural = jnp.concatenate(lanes, axis=0)
        depth = blocks * sub
        lanes_at = min(256, depth)
        line_ = lax.broadcasted_iota(jnp.int32, (depth, lanes_at), 0)
        for n in range(0, depth, lanes_at):
            pick = jnp.where(line_ == target_v[:, n : n + lanes_at], 1.0, 0.0).astype(BF16)
            ordered_v[:, n : n + lanes_at] = contract(natural, pick, ((1,), (0,))).astype(BF16)

    core = lax.rem(t, 2)
    chip = t // 2
    sibling = t + 1 - 2 * core

    def pair_copy(c):
        own = pl.ds(c * band_chips, band_chips)
        return remote(give_v.at[own], take_v.at[own], pair_send.at[c], pair_recv.at[c], (f, sibling))

    def product(c):
        depth = 2 * ny * TILE
        acc = None
        for k in range(nz // 2):
            if c == 0:
                w = w_v[c][2 * k * ny : (2 * k + 2) * ny].reshape(depth, band_chips * 2 * HD)
            else:
                w = jnp.concatenate(
                    [w_v[c][yy * nz + zz] for zz in (2 * k, 2 * k + 1) for yy in range(ny)], axis=0
                )
            term = contract(ordered_v[:, k * depth : (k + 1) * depth], w, ((1,), (0,)))
            acc = term if acc is None else acc + term
        for j in range(band_chips):
            one = acc[:, 2 * j * HD : (2 * j + 1) * HD]
            two = acc[:, (2 * j + 1) * HD : (2 * j + 2) * HD]
            mine_v[c * band_chips + j] = jnp.where(core == 0, one, two)
            give_v[c * band_chips + j] = jnp.where(core == 0, two, one)
        start(pair_copy(c))

    def to_owner(c, dh):
        hh = lax.rem(h + dh, nh)
        return remote(
            out_v.at[c, pl.ds(pl.multiple_of(hh * total, 16), total)],
            part_in_v.at[h * chips + chip],
            p6_send.at[c, dh],
            p6_recv.at[dh * chips + lax.rem(c - chip + chips, chips)],
            at(z, y, hh, 2 * c + core),
        )

    def each_owner(c, act):
        for dh in range(nh):
            if dh:
                act(to_owner(c, dh))
            else:

                @pl.when(chip != c)
                def _():
                    act(to_owner(c, 0))

    def combine(band):
        pair_copy(band).wait_recv()
        for c in range(band * band_chips, (band + 1) * band_chips):
            both = mine_v[c] + take_v[c]
            mine_v[c] = both
            out_v[c] = both.astype(BF16)
            each_owner(c, lambda copy: copy.start())

    steps = max(ny, nz) // 2
    for c in range(bands):
        stage1_wait(c)
    for half in range(CUTS):
        stage2_send(0, half)
    for step in range(1, steps):
        for half in range(CUTS):
            some_cached(-(-packs * (CUTS * (step - 1) + half + 1) // (CUTS * (steps - 1))))
            stage2_wait(step - 1, half)
            stage2_send(step, half)
    some_cached(packs)
    hidden_wait()
    reorder()
    for half in range(CUTS):
        stage2_wait(steps - 1, half)
    for c in range(bands):
        product(c)
    for c in range(bands):
        combine(c)

    keys = mine_v[chip, pl.ds(pl.multiple_of(h * total, 16), total)]
    for dh in range(nh):
        for d in range(chips):
            if (dh, d) != (0, 0):
                source = lax.rem(h + nh - dh, nh) * chips + lax.rem(chip + chips - d, chips)
                into = part_in_v.at[source]
                remote(into, into, p6_send.at[0, 0], p6_recv.at[dh * chips + d], (f, sibling)).wait_recv()
                keys = keys + part_in_v[source].astype(F32)
    keys16 = keys.astype(BF16)
    keys32 = keys16.astype(F32)
    fresh_v[...] = keys32
    keys_ref[0] = keys32[:rows].astype(BF16)
    keys_ref[1] = keys32[rows:].astype(BF16)

    line2 = lax.broadcasted_iota(jnp.int32, (lines, 16), 0)
    place2 = lax.broadcasted_iota(jnp.int32, (lines, 16), 1)
    allowed = (lax.rem(line2, 8) == lax.rem(place2, 8)) & (place2 // 8 <= line2 // (heads * 8))

    def finish(i, carry):
        row = pl.multiple_of(i * 8, 8)
        late = pl.multiple_of(rows + i * 8, 8)
        nk = jnp.concatenate([fresh_v[pl.ds(row, 8)], fresh_v[pl.ds(late, 8)]], axis=0).astype(BF16)
        nv = jnp.concatenate([nval_v[pl.ds(row, 8)], nval_v[pl.ds(late, 8)]], axis=0).astype(BF16)
        scores = jnp.where(allowed, contract(q_v[i], nk, ((1,), (1,))) * factor, NEG)
        old = m_v[i]
        top = jnp.maximum(old, jnp.max(scores, axis=1, keepdims=True))
        keep = jnp.exp(old - top)
        expo = jnp.exp(scores - top[:, :16])
        weight = l_v[i] * keep + jnp.sum(expo, axis=1, keepdims=True)
        out = (o_v[i] * keep + contract(expo.astype(BF16), nv, ((1,), (0,)))) / weight
        for s in range(2):
            for g in range(heads):
                at_line = (s * heads + g) * 8
                result_v[s, pl.ds(row, 8), g * HD : (g + 1) * HD] = out[at_line : at_line + 8]
        return carry

    lax.fori_loop(0, packs, finish, 0)
    attended_ref[...] = result_v[...].astype(BF16)

    for copy in sent:
        copy.wait_send()
    for c in range(chips):
        each_owner(c, lambda copy: copy.wait_send())


def per_device(
    grid,
    nt,
    hidden,
    queries,
    cache_keys,
    cache_values,
    new_values,
    lengths,
    base_weight,
    delta_values,
    delta_scales,
    block_order,
):
    nz, ny, nh = grid
    blocks = nz * ny * nh
    rows = hidden.shape[1]
    blk = base_weight.shape[0] // blocks
    assert blk == nt * TILE and base_weight.shape[1] == HD
    chips = nt // 2
    total = 2 * rows
    assert nh == 2
    span = blocks // nt * TILE // nh
    width = nt * nh * span
    heads = queries.shape[2] // HD
    packs = rows // 8
    lines = 2 * heads * 8
    cap = cache_keys.shape[1]
    ring = max(ny, nz)
    xs = nh * nt - 1
    dma = pltpu.SemaphoreType.DMA
    smem = pltpu.SMEM
    scratch = [
        smem(block_order.shape, jnp.int32),
        smem(lengths.shape, jnp.int32),
        pltpu.VMEM((1, blocks * TILE // nh), jnp.int32),
        pltpu.VMEM((1, 1), BF16),
        pltpu.VMEM((blocks, blk, HD), BF16),
        pltpu.VMEM(delta_values.shape, BF16),
        pltpu.VMEM(new_values.shape, BF16),
        pltpu.VMEM((nt, 2 * TILE, HD), BF16),
        pltpu.VMEM(hidden.shape, BF16),
        pltpu.VMEM(queries.shape, BF16),
        pltpu.VMEM(cache_keys.shape, BF16),
        pltpu.VMEM(cache_values.shape, BF16),
        pltpu.VMEM((total, width), BF16),
        pltpu.VMEM((width, nh * span), BF16),
        pltpu.VMEM((nh * nt, total, span), BF16),
        pltpu.VMEM((nh * nt, total, span), BF16),
        pltpu.VMEM((nh * nt, 2 * TILE, HD), BF16),
        pltpu.VMEM((nh, TILE, nt * HD), BF16),
        pltpu.VMEM(queries.shape, F32),
        *[pltpu.VMEM((blocks // nh, TILE, nt * HD // 2), BF16) for _ in range(2)],
        pltpu.VMEM((nh * total, blocks * TILE // nh), BF16),
        pltpu.VMEM((chips, nh * total, HD), F32),
        pltpu.VMEM((chips, nh * total, HD), F32),
        pltpu.VMEM((chips, nh * total, HD), F32),
        pltpu.VMEM((chips, nh * total, HD), BF16),
        pltpu.VMEM((nh * chips, total, HD), BF16),
        pltpu.VMEM((total, HD), F32),
        pltpu.VMEM((total, HD), F32),
        pltpu.VMEM((packs, lines, HD), BF16),
        pltpu.VMEM((packs, lines, HD), F32),
        pltpu.VMEM((packs, lines, HD), F32),
        pltpu.VMEM((packs, lines, HD), F32),
        pltpu.VMEM((lines, 8 * cap), F32),
        pltpu.VMEM(queries.shape, F32),
        dma((10,)),
        dma((xs,)),
        dma((xs,)),
        dma,
        dma,
        dma((xs,)),
        dma((xs,)),
        dma((2, ring)),
        dma((2, ring)),
        dma((2, 2, ring // 2, CUTS)),
        dma((2, 2, ring // 2, CUTS)),
        dma((2,)),
        dma((2,)),
        dma((chips, nh)),
        dma((nh * chips,)),
    ]
    vmem = pl.BlockSpec(memory_space=pltpu.VMEM)
    hbm = pl.BlockSpec(memory_space=pltpu.HBM)
    return tuple(
        pl.pallas_call(
            functools.partial(kernel, (nz, ny, nh, nt, rows)),
            out_shape=(
                jax.ShapeDtypeStruct(queries.shape, BF16),
                jax.ShapeDtypeStruct((2, rows, HD), BF16),
            ),
            in_specs=[hbm] * 10,
            out_specs=(vmem, vmem),
            scratch_shapes=scratch,
            compiler_params=pltpu.CompilerParams(
                collective_id=0, has_side_effects=True, vmem_limit_bytes=63 * 2**20
            ),
            name="refresh_project_attend",
        )(
            block_order,
            lengths,
            delta_scales,
            base_weight.reshape(blocks, blk, HD),
            delta_values,
            hidden,
            queries,
            cache_keys,
            cache_values,
            new_values,
        )
    )


def solution(mesh, grid=None):
    grid = grid or GRID[mesh.shape["fsdp"]]
    in_specs = (
        P(None, "fsdp", "tp"),
        P(None, "fsdp", "tp"),
        P("fsdp", None, "tp"),
        P("fsdp", None, "tp"),
        P(None, "fsdp", "tp"),
        P("fsdp"),
        P(None, "tp"),
        P(("fsdp", "tp"), None),
        P("fsdp", "tp"),
        P(),
    )
    out_specs = (P(None, "fsdp", "tp"), P(None, "fsdp", "tp"))
    return jax.shard_map(
        functools.partial(per_device, grid, mesh.shape["tp"]),
        mesh=mesh,
        in_specs=in_specs,
        out_specs=out_specs,
        check_vma=False,
    )
```

time: 97.9 us -> 74.4 us (0.76)
  the two profiles are of different devices: /device:TPU:13 before, /device:TPU:15 now
where the time goes in v2:
time: 74.4 us; the launch traced here: 74 us
  Pallas kernels  69.4 us (93%)
  local copies, waits for them, and re-layouts  3.32 us (4%)
  between operations  1.3 us (2%)
    pallas_call x1, Pallas kernels, per_device(): pl.pallas_call(functools.partial(kernel, (nz, ny, nh, nt, rows)), out_sha...  69.4 us
    unnamed x2, local copies, waits for them, and re-layouts  3.32 us

profile of v2, /device:TPU:15, one launch (start us, length us, event | category | flops | bytes accessed | tf_op | source)
XLA Modules:
  0.0 74.0 jit_solution(203036474140266217)
XLA Ops:
  1.3 69.4 %refresh_project_attend.1 = (bf16[2,72,2048]{2,1,0:T(8,128)(2,1)}, bf16[2,72,128]{2,1,0:T(8,128)(2,1)}) custom-call(s32[128]{0:T(128)} %order_hbm.1, s32[72]{0:T(128)} %lengths_hbm.1, bf16[1,1]{1,0:T(2,128)(2,1)S(6)} %copy.14.scale_hbm, bf16[128,128,128]{2,1,0:T(8,128)(2,1)} %bitcast.1, bf16[16,1024]{1,0:T(8,128)(2,1)} %delta_hbm.1, ...), custom_call_target="tpu_custom_call" | custom-call | tf_op jit(solution)/shard_map/refresh_project_attend/pallas_call | solution.py:565
  70.7 1.9 %copy.15 = bf16[2,72,2048]{2,1,0:T(8,128)(2,1)} copy(bf16[2,72,2048]{2,1,0:T(8,128)(2,1)} %get-tuple-element.4) | data formatting | bytes 1179648
  72.6 1.4 %copy.16 = bf16[2,72,128]{2,1,0:T(8,128)(2,1)} copy(bf16[2,72,128]{2,1,0:T(8,128)(2,1)} %get-tuple-element.5) | data formatting | bytes 73728

commit v3 on v2

--- a/solution.py
+++ b/solution.py
@@ -15,7 +15,7 @@
 BF16 = jnp.bfloat16
 GRID = {128: (8, 8, 2)}
 NEG = -1e30
-CUTS = 2
+CUTS = 4
 
 
 def contract(a, b, dims):
@@ -144,7 +144,7 @@
             )
         )
     ]
-    for load in loads:
+    for load in loads[:4]:
         load.start()
 
     barrier = pltpu.get_barrier_semaphore()
@@ -158,6 +158,8 @@
         count += 1
     for load in loads[:4]:
         load.wait()
+    for load in loads[4:]:
+        load.start()
     parcel_ref[:, :TILE] = base_v[order_ref[f]].reshape(nt, TILE, HD)
     parcel_ref[:, TILE:] = jnp.broadcast_to(scale_v[...].reshape(1, 1, 1), (nt, TILE, HD))
     pl.semaphore_wait(barrier, count)
@@ -188,6 +190,87 @@
     parcels_v[h * nt + t] = parcel_ref[t]
     deltas_v[h] = delta_ref[...]
 
+    def hidden_wait():
+        for i, (dh, d) in enumerate(x_peers):
+            source = lax.rem(h + nh - dh, nh) * nt + lax.rem(t + nt - d, nt)
+            remote(regroup_v.at[0], hid_v.at[source], hid_send.at[i], hid_recv.at[i], x_peer(dh, d)).wait_recv()
+
+    for i, (dh, d) in enumerate(x_peers):
+        source = lax.rem(h + nh - dh, nh) * nt + lax.rem(t + nt - d, nt)
+        remote(parcel_ref.at[0], parcels_v.at[source], p0_send.at[i], p0_recv.at[i], x_peer(dh, d)).wait_recv()
+    if nh > 1:
+        remote(delta_ref, deltas_v.at[1 - h], delta_send, delta_recv, x_peer(1, 0)).wait_recv()
+
+    def axes(c):
+        if c == 0:
+            return (y, ny, y_peer), (z, nz, z_peer)
+        return (z, nz, z_peer), (y, ny, y_peer)
+
+    def half_of(rows16):
+        out = rows16[:sub]
+        for hh in range(1, nh):
+            out = jnp.where(h == hh, rows16[hh * sub : (hh + 1) * sub], out)
+        return out
+
+    for c in range(bands):
+        (a, na, _), (b, nb, _) = axes(c)
+        cols = []
+        for col in range(c * nt // bands, (c + 1) * nt // bands):
+            parts = []
+            for hh in range(nh):
+                parcel = parcels_v[hh * nt + col].astype(F32)
+                update = deltas_v[hh, :, col * HD : (col + 1) * HD].astype(F32)
+                scaled = (half_of(update) * parcel[TILE : TILE + sub]).astype(BF16).astype(F32)
+                parts.append(half_of(parcel[:TILE]) + scaled)
+            cols.append(jnp.concatenate(parts, axis=0))
+        w_v[c][b * na + a] = jnp.concatenate(cols, axis=1).astype(BF16)
+
+    def stage1_piece(c, source_a):
+        (a, na, _), (b, nb, _) = axes(c)
+        return w_v[c].at[pl.ds(b * na + source_a, 1)]
+
+    def stage1_send(c):
+        (a, na, peer), _ = axes(c)
+        for s in range(1, na):
+            start(remote(stage1_piece(c, a), stage1_piece(c, a), s1_send.at[c, s], s1_recv.at[c, s], peer(s)))
+
+    def stage1_wait(c):
+        (a, na, peer), _ = axes(c)
+        for s in range(1, na):
+            piece = stage1_piece(c, lax.rem(a + na - s, na))
+            remote(piece, piece, s1_send.at[c, s], s1_recv.at[c, s], peer(s)).wait_recv()
+
+    def unit(c, which, half):
+        (a, na, _), (b, nb, _) = axes(c)
+        size = na // CUTS
+        start_row = lax.rem(b + which + 2 * nb, nb) * na + half * size
+        return w_v[c].at[pl.ds(start_row, size)]
+
+    def hops(c, way, half):
+        nb = axes(c)[1][1]
+        return nb // 2 if (half < CUTS // 2) == (way == 0) else nb - 1 - nb // 2
+
+    def stage2_each(step, half, ahead, act):
+        for c in range(bands):
+            peer = axes(c)[1][2]
+            for way, sign in enumerate((1, -1)):
+                if step < hops(c, way, half):
+                    piece = unit(c, -sign * (step + ahead), half)
+                    act(
+                        remote(
+                            piece, piece, s2_send.at[c, way, step, half], s2_recv.at[c, way, step, half], peer(sign)
+                        )
+                    )
+
+    def stage2_send(step, half):
+        stage2_each(step, half, 0, start)
+
+    def stage2_wait(step, half):
+        stage2_each(step, half, 1, lambda copy: copy.wait_recv())
+
+    for c in range(bands):
+        stage1_send(c)
+
     lane_k = lax.broadcasted_iota(jnp.int32, (width, nh * span), 0)
     lane_l = lax.broadcasted_iota(jnp.int32, (width, nh * span), 1)
     target = lax.rem(lane_k, TILE) // sub * span + lane_k // (nt * TILE) * sub + lax.rem(lane_k, sub)
@@ -215,87 +298,6 @@
             )
         )
     hid_v[h * nt + t] = regroup_v[h * nt + t]
-
-    def hidden_wait():
-        for i, (dh, d) in enumerate(x_peers):
-            source = lax.rem(h + nh - dh, nh) * nt + lax.rem(t + nt - d, nt)
-            remote(regroup_v.at[0], hid_v.at[source], hid_send.at[i], hid_recv.at[i], x_peer(dh, d)).wait_recv()
-
-    for i, (dh, d) in enumerate(x_peers):
-        source = lax.rem(h + nh - dh, nh) * nt + lax.rem(t + nt - d, nt)
-        remote(parcel_ref.at[0], parcels_v.at[source], p0_send.at[i], p0_recv.at[i], x_peer(dh, d)).wait_recv()
-    if nh > 1:
-        remote(delta_ref, deltas_v.at[1 - h], delta_send, delta_recv, x_peer(1, 0)).wait_recv()
-
-    def axes(c):
-        if c == 0:
-            return (y, ny, y_peer), (z, nz, z_peer)
-        return (z, nz, z_peer), (y, ny, y_peer)
-
-    def half_of(rows16):
-        out = rows16[:sub]
-        for hh in range(1, nh):
-            out = jnp.where(h == hh, rows16[hh * sub : (hh + 1) * sub], out)
-        return out
-
-    for c in range(bands):
-        (a, na, _), (b, nb, _) = axes(c)
-        cols = []
-        for col in range(c * nt // bands, (c + 1) * nt // bands):
-            parts = []
-            for hh in range(nh):
-                parcel = parcels_v[hh * nt + col].astype(F32)
-                update = deltas_v[hh, :, col * HD : (col + 1) * HD].astype(F32)
-                scaled = (half_of(update) * parcel[TILE : TILE + sub]).astype(BF16).astype(F32)
-                parts.append(half_of(parcel[:TILE]) + scaled)
-            cols.append(jnp.concatenate(parts, axis=0))
-        w_v[c][b * na + a] = jnp.concatenate(cols, axis=1).astype(BF16)
-
-    def stage1_piece(c, source_a):
-        (a, na, _), (b, nb, _) = axes(c)
-        return w_v[c].at[pl.ds(b * na + source_a, 1)]
-
-    def stage1_send(c):
-        (a, na, peer), _ = axes(c)
-        for s in range(1, na):
-            start(remote(stage1_piece(c, a), stage1_piece(c, a), s1_send.at[c, s], s1_recv.at[c, s], peer(s)))
-
-    def stage1_wait(c):
-        (a, na, peer), _ = axes(c)
-        for s in range(1, na):
-            piece = stage1_piece(c, lax.rem(a + na - s, na))
-            remote(piece, piece, s1_send.at[c, s], s1_recv.at[c, s], peer(s)).wait_recv()
-
-    def unit(c, which, half):
-        (a, na, _), (b, nb, _) = axes(c)
-        size = na // CUTS
-        start_row = lax.rem(b + which + 2 * nb, nb) * na + half * size
-        return w_v[c].at[pl.ds(start_row, size)]
-
-    def hops(c, way, half):
-        nb = axes(c)[1][1]
-        return nb // 2 if (half < CUTS // 2) == (way == 0) else nb - 1 - nb // 2
-
-    def stage2_each(step, half, ahead, act):
-        for c in range(bands):
-            peer = axes(c)[1][2]
-            for way, sign in enumerate((1, -1)):
-                if step < hops(c, way, half):
-                    piece = unit(c, -sign * (step + ahead), half)
-                    act(
-                        remote(
-                            piece, piece, s2_send.at[c, way, step, half], s2_recv.at[c, way, step, half], peer(sign)
-                        )
-                    )
-
-    def stage2_send(step, half):
-        stage2_each(step, half, 0, start)
-
-    def stage2_wait(step, half):
-        stage2_each(step, half, 1, lambda copy: copy.wait_recv())
-
-    for c in range(bands):
-        stage1_send(c)
 
     for load in loads[5:]:
         load.wait()
@@ -474,6 +476,22 @@
         copy.wait_send()
     for c in range(chips):
         each_owner(c, lambda copy: copy.wait_send())
+
+
+def hand_over(attended_in, keys_in, attended_out, keys_out, attended_v, keys_v, in_sem, out_sem):
+    half = attended_in.shape[2] // 2
+    spans = [(s, slice(None), pl.ds(k * half, half)) for s in range(2) for k in range(2)]
+    routes = [(keys_in, keys_v, keys_out)]
+    routes += [(attended_in.at[span], attended_v.at[span], attended_out.at[span]) for span in spans]
+    into = [pltpu.make_async_copy(r[0], r[1], in_sem.at[i]) for i, r in enumerate(routes)]
+    out = [pltpu.make_async_copy(r[1], r[2], out_sem.at[i]) for i, r in enumerate(routes)]
+    for copy in into:
+        copy.start()
+    for arrived, copy in zip(into, out):
+        arrived.wait()
+        copy.start()
+    for copy in out:
+        copy.wait()
 
 
 def per_device(
@@ -561,7 +579,7 @@
     ]
     vmem = pl.BlockSpec(memory_space=pltpu.VMEM)
     hbm = pl.BlockSpec(memory_space=pltpu.HBM)
-    return tuple(
+    results = tuple(
         pl.pallas_call(
             functools.partial(kernel, (nz, ny, nh, nt, rows)),
             out_shape=(
@@ -588,6 +606,15 @@
             new_values,
         )
     )
+    return pl.pallas_call(
+        hand_over,
+        out_shape=tuple(jax.ShapeDtypeStruct(r.shape, r.dtype) for r in results),
+        in_specs=[hbm] * 2,
+        out_specs=(hbm, hbm),
+        scratch_shapes=[pltpu.VMEM(r.shape, r.dtype) for r in results] + [dma((5,)), dma((5,))],
+        compiler_params=pltpu.CompilerParams(vmem_limit_bytes=63 * 2**20),
+        name="hand_over",
+    )(*results)
 
 
 def solution(mesh, grid=None):

time: 74.4 us -> 71.7 us (0.964)
  local copies, waits for them, and re-layouts: 3.32 us -> 0 us
  Pallas kernels: 69.4 us -> 70.3 us
    unnamed x2 -> x0, local copies, waits for them, and re-layouts: 3.32 us -> none
    pallas_call x0 -> x1, Pallas kernels: none -> 1.89 us  [per_device(): pl.pallas_call(hand_over, out_shape=tuple((jax.ShapeDtypeStruct(r.shape,...]
    pallas_call x1, Pallas kernels: 69.4 us -> 68.4 us  [per_device(): pl.pallas_call(functools.partial(kernel, (nz, ny, nh, nt, rows)), out_sha...]
where the time goes in v3:
time: 71.7 us; the launch traced here: 71.6 us
  Pallas kernels  70.3 us (98%)
  between operations  1.3 us (2%)
    pallas_call x1, Pallas kernels, per_device(): pl.pallas_call(functools.partial(kernel, (nz, ny, nh, nt, rows)), out_sha...  68.4 us
    pallas_call x1, Pallas kernels, per_device(): pl.pallas_call(hand_over, out_shape=tuple((jax.ShapeDtypeStruct(r.shape,...  1.89 us

profile of v3, /device:TPU:15, one launch (start us, length us, event | category | flops | bytes accessed | tf_op | source)
XLA Modules:
  0.0 71.6 jit_solution(13439114438066164583)
XLA Ops:
  1.3 68.4 %refresh_project_attend.1 = (bf16[2,72,2048]{2,1,0:T(8,128)(2,1)}, bf16[2,72,128]{2,1,0:T(8,128)(2,1)}) custom-call(s32[128]{0:T(128)} %order_hbm.1, s32[72]{0:T(128)} %lengths_hbm.1, bf16[1,1]{1,0:T(2,128)(2,1)S(6)} %copy.12.scale_hbm, bf16[128,128,128]{2,1,0:T(8,128)(2,1)} %bitcast.1, bf16[16,1024]{1,0:T(8,128)(2,1)} %delta_hbm.1, ...), custom_call_target="tpu_custom_call" | custom-call | tf_op jit(solution)/shard_map/refresh_project_attend/pallas_call | solution.py:583
  69.7 1.9 %hand_over.1 = (bf16[2,72,2048]{2,1,0:T(8,128)(2,1)}, bf16[2,72,128]{2,1,0:T(8,128)(2,1)}) custom-call(bf16[2,72,2048]{2,1,0:T(8,128)(2,1)} %get-tuple-element.4.attended_in, bf16[2,72,128]{2,1,0:T(8,128)(2,1)} %get-tuple-element.5.keys_in), custom_call_target="tpu_custom_call" | custom-call | tf_op jit(solution)/shard_map/hand_over/pallas_call | solution.py:609

commit v4 on v3

--- a/solution.py
+++ b/solution.py
@@ -469,7 +469,7 @@
                 result_v[s, pl.ds(row, 8), g * HD : (g + 1) * HD] = out[at_line : at_line + 8]
         return carry
 
-    lax.fori_loop(0, packs, finish, 0)
+    lax.fori_loop(0, packs, finish, 0, unroll=3)
     attended_ref[...] = result_v[...].astype(BF16)
 
     for copy in sent:

time: 71.7 us -> 70.5 us (0.983)
  Pallas kernels: 70.3 us -> 69 us
    pallas_call x1, Pallas kernels: 68.4 us -> 67.1 us  [per_device(): pl.pallas_call(functools.partial(kernel, (nz, ny, nh, nt, rows)), out_sha...]
where the time goes in v4:
time: 70.5 us; the launch traced here: 70.3 us
  Pallas kernels  69 us (98%)
  between operations  1.3 us (2%)
    pallas_call x1, Pallas kernels, per_device(): pl.pallas_call(functools.partial(kernel, (nz, ny, nh, nt, rows)), out_sha...  67.1 us
    pallas_call x1, Pallas kernels, per_device(): pl.pallas_call(hand_over, out_shape=tuple((jax.ShapeDtypeStruct(r.shape,...  1.89 us

profile of v4, /device:TPU:15, one launch (start us, length us, event | category | flops | bytes accessed | tf_op | source)
XLA Modules:
  0.0 70.3 jit_solution(8461455862866442895)
XLA Ops:
  1.3 67.1 %refresh_project_attend.1 = (bf16[2,72,2048]{2,1,0:T(8,128)(2,1)}, bf16[2,72,128]{2,1,0:T(8,128)(2,1)}) custom-call(s32[128]{0:T(128)} %order_hbm.1, s32[72]{0:T(128)} %lengths_hbm.1, bf16[1,1]{1,0:T(2,128)(2,1)S(6)} %copy.12.scale_hbm, bf16[128,128,128]{2,1,0:T(8,128)(2,1)} %bitcast.1, bf16[16,1024]{1,0:T(8,128)(2,1)} %delta_hbm.1, ...), custom_call_target="tpu_custom_call" | custom-call | tf_op jit(solution)/shard_map/refresh_project_attend/pallas_call | solution.py:583
  68.4 1.9 %hand_over.1 = (bf16[2,72,2048]{2,1,0:T(8,128)(2,1)}, bf16[2,72,128]{2,1,0:T(8,128)(2,1)}) custom-call(bf16[2,72,2048]{2,1,0:T(8,128)(2,1)} %get-tuple-element.4.attended_in, bf16[2,72,128]{2,1,0:T(8,128)(2,1)} %get-tuple-element.5.keys_in), custom_call_target="tpu_custom_call" | custom-call | tf_op jit(solution)/shard_map/hand_over/pallas_call | solution.py:609
